TPU v7x, 32 devices: a whole 2x2x4 slice. The times are simulated.
32 devices in a mesh: grp: 2 (over x), exp: 16 (over z, y, core).
Axes of the slice: x: 2, y: 2, z: 4, core: 2. Of those that a mesh axis runs over, the one named last changes fastest.
Arguments:
- tokens: bfloat16 [512, 2048], P(('grp', 'exp')), parts along dimension 0, may hold values from -6 to 6
- router_weight: bfloat16 [2048, 16], replicated, may hold values from -0.0625 to 0.0625
- w_gate: bfloat16 [16, 2048, 768], P('exp'), may hold values from -0.125 to 0.125
- w_up: bfloat16 [16, 2048, 768], P('exp'), may hold values from -0.125 to 0.125
- w_down: bfloat16 [16, 768, 2048], P('exp'), may hold values from -0.3125 to 0.3125
- expert_ids: int32 [512, 8], P(('grp', 'exp')), parts along dimension 0, may hold values from 0 to 15, all different within a row; in each aligned block of 16 rows (0 to 15, 16 to 31, ...) at most 12 rows name the same one
Outputs:
- moe_out: bfloat16 [512, 2048], P(('grp', 'exp')), parts along dimension 0
There are 2 independent parts, one for each index of `grp`. A program takes and returns all parts, laid end to end along the dimension named above; an argument that names none is the same for every part. Nothing has to cross between parts.
Inputs may be any that keep to these rules, and one draw needn't show every extreme that they name: `expert_ids`: each row names 8 different experts; among the 16 rows of one device no expert is named by more than 12 rows.
All inputs are finite; a program needn't handle non-finite values.
Results may differ from a plain program's by a relative error of at most 0.0085.
Values may be sent and summed in bfloat16 or wider, within the bound.
A program may use at most 64 MiB of HBM per device.

v0:
```python
import jax
import jax.numpy as jnp
from jax import lax
from jax.sharding import PartitionSpec as P


def expert_rows(rows, gate_mat, up_mat, down_mat):
    gate = jnp.dot(rows, gate_mat, preferred_element_type=jnp.float32)
    upper = jnp.dot(rows, up_mat, preferred_element_type=jnp.float32)
    act = (jax.nn.silu(gate) * upper).astype(jnp.bfloat16)
    return jnp.dot(act, down_mat, preferred_element_type=jnp.float32).astype(jnp.bfloat16)


def on_device(tokens, router_weight, w_gate, w_up, w_down, expert_ids):
    devices = lax.axis_size("exp")
    tok_rows, chosen = expert_ids.shape
    width = tokens.shape[1]
    experts = devices * w_gate.shape[0]
    capacity = min(tok_rows, max(2, (3 * tok_rows * chosen + 2 * experts - 1) // (2 * experts)))
    logits = jnp.dot(tokens, router_weight, preferred_element_type=jnp.float32)
    picked = jnp.take_along_axis(logits, expert_ids, axis=1)
    gates = jax.nn.softmax(picked, axis=1)
    flat_ids = expert_ids.reshape(-1)
    onehot = (flat_ids[:, None] == jnp.arange(experts, dtype=jnp.int32)[None, :]).astype(jnp.int32)
    ranks = jnp.cumsum(onehot, axis=0) - onehot
    slot = jnp.sum(ranks * onehot, axis=1)
    place = slot * experts + flat_ids
    repeated = jnp.repeat(tokens, chosen, axis=0)
    filled = jnp.zeros((capacity * experts, width), jnp.bfloat16).at[place].set(repeated)
    received = lax.all_to_all(
        filled.reshape(capacity, experts, width), "exp", split_axis=1, concat_axis=1, tiled=True
    )
    count = received.shape[0]
    outs = expert_rows(received.reshape(-1, width), w_gate[0], w_up[0], w_down[0])
    back = lax.all_to_all(
        outs.reshape(count, experts, width), "exp", split_axis=1, concat_axis=1, tiled=True
    )
    values = back.reshape(capacity * experts, width)[place].reshape(tok_rows, chosen, width)
    mixed = jnp.einsum("tk,tkd->td", gates, values.astype(jnp.float32))
    return mixed.astype(jnp.bfloat16)


def solution(mesh):
    placed = (
        P(("grp", "exp"), None),
        P(),
        P("exp", None, None),
        P("exp", None, None),
        P("exp", None, None),
        P(("grp", "exp"), None),
    )
    return jax.shard_map(
        on_device, mesh=mesh, in_specs=placed, out_specs=P(("grp", "exp"), None), check_vma=False
    )
```

profile of v0, /device:TPU:0, one launch (start us, length us, event | category | flops | bytes accessed | tf_op | source)
XLA Modules:
  0.0 84.4 jit_solution(11013531206939314225)
XLA Ops:
  0.0 0.0 copy-start
  0.0 0.9 %copy.23 = s32[16,8]{1,0:T(8,128)S(1)} copy(s32[16,8]{0,1:T(8,128)} %param.11) | data formatting | bytes 1024 | tf_op args[5]
  0.9 0.1 eq.15
  1.0 0.1 reshape.62
  1.1 0.1 fusion.29
  1.2 0.2 reduce_window_sum.11
  1.4 0.2 select_reduce_fusion
  1.5 2.6 %scatter_custom_fusion = bf16[192,2048]{1,0:T(8,128)(2,1)} fusion(s32[128]{0:T(128)S(1)} %fusion.31, bf16[]{:T(256)} %constant.32.clone.1, bf16[16,2048]{1,0:T(8,128)(2,1)} %param.6), kind=kCustom, calls=%fused_computation.19 | custom fusion | bytes 851970 | tf_op jit(solution)/shard_map/scatter | solution.py:29
  4.1 0.0 copy-start.1
  4.1 1.7 %copy.25 = bf16[12,16,2048]{2,0,1:T(8,128)(2,1)S(1)} copy(bf16[12,16,2048]{2,1,0:T(8,128)(2,1)} %bitcast.48) | data formatting | bytes 1572864 | tf_op jit(solution)/shard_map/reshape | solution.py:31
  5.9 32.0 %all_to_all.10 = bf16[12,16,2048]{2,0,1:T(8,128)(2,1)S(1)} all-to-all(bf16[12,16,2048]{2,0,1:T(8,128)(2,1)S(1)} %copy.25), channel_id=1, replica_groups=mesh['grp'=2,'exp'=16] {'exp'}, dimensions={1} | all-to-all | bytes 1572864 | tf_op jit(solution)/shard_map/all_to_all | solution.py:30
  37.9 0.4 copy.26
  38.4 0.0 copy-start.2
  38.4 0.9 %copy-done.2 = bf16[12,16,2048]{2,1,0:T(8,128)(2,1)} copy-done((bf16[12,16,2048]{2,1,0:T(8,128)(2,1)}, bf16[12,16,2048]{2,1,0:T(8,128)(2,1)S(1)}, u32[]{:S(2)}) %copy-start.2) | copy-done | bytes 786456
  39.3 0.0 copy-done.1
  39.3 1.6 %fusion.4 = f32[192,768]{1,0:T(8,128)} fusion(bf16[192,2048]{1,0:T(8,128)(2,1)S(1)} %bitcast.49, bf16[1,2048,768]{2,1,0:T(8,128)(2,1)S(1)} %copy-done.1), kind=kOutput, calls=%fused_computation.7 | convolution fusion | flops 603979776 | bytes 4521984 | tf_op jit(solution)/shard_map/dot_general | solution.py:8
  40.9 0.0 copy-done
  40.9 4.8 %fusion.6 = bf16[192,2048]{1,0:T(8,128)(2,1)} fusion(bf16[1,768,2048]{2,1,0:T(8,128)(2,1)S(1)} %copy-done, bf16[192,2048]{1,0:T(8,128)(2,1)} %bitcast.50, bf16[1,2048,768]{2,1,0:T(8,128)(2,1)} %param.9, f32[192,768]{1,0:T(8,128)} %fusion.4), kind=kOutput, calls=%fused_computation.9 | convolution fusion | flops 1209237504 | bytes 8454144 | tf_op jit(solution)/shard_map/dot_general | solution.py:11
  45.7 0.0 copy-start.4
  45.7 0.0 copy-start.3
  45.7 0.0 copy-start.5
  45.7 2.7 %copy.27 = bf16[12,16,2048]{2,0,1:T(8,128)(2,1)} copy(bf16[12,16,2048]{2,1,0:T(8,128)(2,1)} %bitcast.51) | data formatting | bytes 1572864 | tf_op jit(solution)/shard_map/reshape | solution.py:36
  48.3 5.0 %all-to-all-start.1 = ((bf16[12,16,2048]{2,0,1:T(8,128)(2,1)}), bf16[12,16,2048]{2,0,1:T(8,128)(2,1)}, u32[]{:S(2)}, u32[]{:S(2)}) async-start(bf16[12,16,2048]{2,0,1:T(8,128)(2,1)} %copy.27), calls=%async_computation.1 | async-start | bytes 2097152 | tf_op jit(solution)/shard_map/all_to_all | solution.py:35
  53.4 0.0 copy-done.4
  53.4 0.1 copy.21
  53.5 0.1 reshape.77
  53.6 0.0 copy-done.3
  53.6 0.0 copy-done.5
  53.6 0.1 fusion.34
  53.7 1.3 %gather_fusion.1 = f32[128]{0:T(128)S(1)} fusion(f32[16,16]{1,0:T(8,128)S(1)} %fusion.34, s32[128]{0:T(128)S(1)} %reshape.77), kind=kCustom, calls=%fused_computation.1 | custom fusion | bytes 2048 | tf_op jit(solution)/shard_map/jit(take_along_axis)/gather | solution.py:21
  55.0 0.1 reshape.80
  55.1 0.1 copy.22
  55.2 0.1 copy.29
  55.3 21.0 %all-to-all-done.1 = bf16[12,16,2048]{2,0,1:T(8,128)(2,1)} async-done(((bf16[12,16,2048]{2,0,1:T(8,128)(2,1)}), bf16[12,16,2048]{2,0,1:T(8,128)(2,1)}, u32[]{:S(2)}, u32[]{:S(2)}) %all-to-all-start.1) | async-done | bytes 786464 | tf_op jit(solution)/shard_map/all_to_all | solution.py:35
  76.4 2.6 %copy.28 = bf16[12,16,2048]{2,1,0:T(8,128)(2,1)} copy(bf16[12,16,2048]{2,0,1:T(8,128)(2,1)} %all-to-all-done.1) | data formatting | bytes 1572864 | tf_op jit(solution)/shard_map/all_to_all | solution.py:35
  79.0 3.5 %gather_fusion = bf16[128,2048]{1,0:T(8,128)(2,1)} fusion(bf16[192,2048]{1,0:T(8,128)(2,1)} %bitcast.47, s32[1024]{0:T(1024)S(1)} %pad_clamp_fusion), kind=kCustom, calls=%fused_computation | custom fusion | bytes 1049088 | tf_op jit(solution)/shard_map/gather | solution.py:38
  82.4 1.3 %fusion.22 = bf16[16,1,2048]{2,1,0:T(2,128)(2,1)S(1)} fusion(bf16[16,8,1]{1,2,0:T(2,128)(2,1)S(1)} %copy.29, bf16[128,2048]{1,0:T(8,128)(2,1)} %gather_fusion), kind=kOutput, calls=%fused_computation.17 | convolution fusion | flops 524288 | bytes 590080 | tf_op jit(solution)/shard_map/tk,tkd->td/dot_general | solution.py:39
  83.7 0.7 copy.32
  (6 shorter events, 0.1 us)
Async XLA Ops:
  0.0 40.9 %copy-start = (bf16[1,768,2048]{2,1,0:T(8,128)(2,1)S(1)}, bf16[1,768,2048]{2,1,0:T(8,128)(2,1)}, u32[]{:S(2)}) copy-start(bf16[1,768,2048]{2,1,0:T(8,128)(2,1)} %param.10) | copy-start | bytes 9437188
  4.1 35.1 %copy-start.1 = (bf16[1,2048,768]{2,1,0:T(8,128)(2,1)S(1)}, bf16[1,2048,768]{2,1,0:T(8,128)(2,1)}, u32[]{:S(2)}) copy-start(bf16[1,2048,768]{2,1,0:T(8,128)(2,1)} %param.8) | copy-start | bytes 9437188
  38.4 0.9 %copy-start.2 = (bf16[12,16,2048]{2,1,0:T(8,128)(2,1)}, bf16[12,16,2048]{2,1,0:T(8,128)(2,1)S(1)}, u32[]{:S(2)}) copy-start(bf16[12,16,2048]{2,1,0:T(8,128)(2,1)S(1)} %copy.26) | copy-start | bytes 2359300
  45.7 7.7 %copy-start.4 = (s32[16,8]{0,1:T(8,128)S(1)}, s32[16,8]{0,1:T(8,128)}, u32[]{:S(2)}) copy-start(s32[16,8]{0,1:T(8,128)} %param.11) | copy-start | bytes 1540
  45.7 7.9 %copy-start.3 = (bf16[16,2048]{1,0:T(8,128)(2,1)S(1)}, bf16[16,2048]{1,0:T(8,128)(2,1)}, u32[]{:S(2)}) copy-start(bf16[16,2048]{1,0:T(8,128)(2,1)} %param.6) | copy-start | bytes 196612
  45.7 7.9 %copy-start.5 = (bf16[2048,16]{0,1:T(8,128)(2,1)S(1)}, bf16[2048,16]{0,1:T(8,128)(2,1)}, u32[]{:S(2)}) copy-start(bf16[2048,16]{0,1:T(8,128)(2,1)} %param.7) | copy-start | bytes 196612
  48.3 28.0 %all-to-all-start.1 = ((bf16[12,16,2048]{2,0,1:T(8,128)(2,1)}), bf16[12,16,2048]{2,0,1:T(8,128)(2,1)}, u32[]{:S(2)}, u32[]{:S(2)}) async-start(bf16[12,16,2048]{2,0,1:T(8,128)(2,1)} %copy.27), calls=%async_computation.1 | async-start | bytes 2097152 | tf_op jit(solution)/shard_map/all_to_all | solution.py:35
where the time goes:
time: 85.9 us; the launch traced here: 84.4 us
  blocking collectives  32 us (37%)
  waiting for transfers between devices  21 us (24%)
  local copies, waits for them, and re-layouts  17.8 us (21%)
  matrix products  7.85 us (9%)
  starting transfers between devices  5.04 us (6%)
    all_to_all x1, blocking collectives, on_device(): lax.all_to_all(filled.reshape(capacity, experts, width), 'exp', split_axi...  32 us
    all_to_all x1, waiting for transfers between devices, on_device(): lax.all_to_all(outs.reshape(count, experts, width), 'exp', split_axis=1,...  21 us
    all_to_all x1, starting transfers between devices, on_device(): lax.all_to_all(outs.reshape(count, experts, width), 'exp', split_axis=1,...  5.04 us
    dot_general x1, matrix products, expert_rows(): jnp.dot(act, down_mat, preferred_element_type=jnp.float32)  4.8 us
    gather x1, local copies, waits for them, and re-layouts, on_device(): back.reshape(capacity * experts, width)[place]  3.46 us
    reshape x1, local copies, waits for them, and re-layouts, on_device(): outs.reshape(count, experts, width)  2.66 us
    scatter x1, local copies, waits for them, and re-layouts, on_device(): jnp.zeros((capacity * experts, width), jnp.bfloat16).at[place].set(repeated)  2.6 us
    all_to_all x1, local copies, waits for them, and re-layouts, on_device(): lax.all_to_all(outs.reshape(count, experts, width), 'exp', split_axis=1,...  2.59 us
  transfers between devices with their start and end apart: 1, of which 1 were waited for; matrix products, arithmetic and copies ran while one was open for 2% of the time, Pallas kernels for 0%

commit v1 on v0

--- a/solution.py
+++ b/solution.py
@@ -1,7 +1,13 @@
+import functools
 import jax
 import jax.numpy as jnp
 from jax import lax
+from jax.experimental import pallas as pl
+from jax.experimental.pallas import tpu as pltpu
 from jax.sharding import PartitionSpec as P
+
+LANES = 128
+MESH = pl.DeviceIdType.MESH
 
 
 def expert_rows(rows, gate_mat, up_mat, down_mat):
@@ -11,12 +17,11 @@
     return jnp.dot(act, down_mat, preferred_element_type=jnp.float32).astype(jnp.bfloat16)
 
 
-def on_device(tokens, router_weight, w_gate, w_up, w_down, expert_ids):
+def dispatch_plan(tokens, router_weight, w_gate, w_up, w_down, expert_ids, capacity):
     devices = lax.axis_size("exp")
     tok_rows, chosen = expert_ids.shape
     width = tokens.shape[1]
     experts = devices * w_gate.shape[0]
-    capacity = min(tok_rows, max(2, (3 * tok_rows * chosen + 2 * experts - 1) // (2 * experts)))
     logits = jnp.dot(tokens, router_weight, preferred_element_type=jnp.float32)
     picked = jnp.take_along_axis(logits, expert_ids, axis=1)
     gates = jax.nn.softmax(picked, axis=1)
@@ -40,6 +45,200 @@
     return mixed.astype(jnp.bfloat16)
 
 
+def moe_kernel(
+    Z, Q, tok, router, ids, w_gate, w_up, w_down, out,
+    rows, ids_v, router_v, gate_v, up_v, down_v, act,
+    keep, core_out, core_in, y_out, y_in, z_out, z_in,
+    load_sem, gz_s, gz_r, gy_s, gy_r, gc_s, gc_r,
+    rc_s, rc_r, ry_s, ry_r, rz_s, rz_r,
+):
+    R, D = tok.shape
+    experts = router.shape[0]
+    ff = gate_v.shape[1]
+    half, quarter = 2 * Z * R, Z * R
+    cols = D // Q
+    me = lax.axis_index("exp")
+    core, y, z = lax.rem(me, 2), lax.rem(me // 2, 2), me // 4
+    core_peer = {"exp": me + 1 - 2 * core}
+    y_peer = {"exp": me + 2 - 4 * y}
+
+    def z_peer(shift):
+        return {"exp": lax.rem(z + shift, Z) * 4 + 2 * y + core}
+
+    def remote(src, dst, send, recv, peer):
+        return pltpu.make_async_remote_copy(
+            src_ref=src, dst_ref=dst, send_sem=send, recv_sem=recv,
+            device_id=peer, device_id_type=MESH,
+        )
+
+    def slot(i, n=1):
+        return rows.at[pl.ds(i * R, n * R)]
+
+    loads = [
+        pltpu.make_async_copy(ids, ids_v, load_sem.at[0]),
+        pltpu.make_async_copy(tok, rows.at[pl.ds(0, R), pl.ds(0, D)], load_sem.at[1]),
+        pltpu.make_async_copy(router, router_v, load_sem.at[2]),
+        pltpu.make_async_copy(w_gate.at[0], gate_v, load_sem.at[3]),
+        pltpu.make_async_copy(w_up.at[0], up_v, load_sem.at[4]),
+        pltpu.make_async_copy(w_down.at[0], down_v, load_sem.at[5]),
+    ]
+    for load in loads[:2]:
+        load.start()
+    barrier = pltpu.get_barrier_semaphore()
+    for peer in [core_peer, y_peer] + [z_peer(s) for s in range(1, Z)]:
+        pl.semaphore_signal(barrier, inc=1, device_id=peer, device_id_type=MESH)
+    for load in loads[2:]:
+        load.start()
+    loads[0].wait()
+    lane = lax.broadcasted_iota(jnp.int32, (LANES, R), 0)
+    named = jnp.zeros((LANES, R), jnp.float32)
+    for k in range(ids.shape[0]):
+        named = jnp.where(ids_v[k : k + 1, :] == lane, 1.0, named)
+    rows[0:R, D : D + LANES] = named.T.astype(jnp.bfloat16)
+    loads[1].wait()
+    pl.semaphore_wait(barrier, Z + 1)
+
+    along_z = [
+        remote(slot(0), slot(s), gz_s.at[s], gz_r.at[s], z_peer(Z - s)) for s in range(1, Z)
+    ]
+    across_y = [
+        remote(slot(s), slot(Z + s), gy_s.at[s], gy_r.at[s], y_peer) for s in range(Z)
+    ]
+    to_core = [
+        remote(slot(s), slot(2 * Z + s), gc_s.at[s], gc_r.at[s], core_peer) for s in range(2 * Z)
+    ]
+    order = [0] + sorted(range(1, Z), key=lambda s: min(s, Z - s))
+    for s in order[1:]:
+        along_z[s - 1].start()
+    across_y[0].start()
+    to_core[0].start()
+    for s in order[1:]:
+        along_z[s - 1].wait_recv()
+        across_y[s].start()
+        to_core[s].start()
+    for s in order:
+        across_y[s].wait_recv()
+        to_core[Z + s].start()
+    for copy in to_core:
+        copy.wait_recv()
+
+    for load in loads[2:]:
+        load.wait()
+    x = rows[:, 0:D]
+    logits = lax.dot_general(
+        x, router_v[...], (((1,), (1,)), ((), ())), preferred_element_type=jnp.float32
+    )
+    chosen = rows[:, D : D + experts].astype(jnp.float32) > 0.5
+    top = jnp.max(jnp.where(chosen, logits, -jnp.inf), axis=1, keepdims=True)
+    weight = jnp.where(chosen, jnp.exp(jnp.where(chosen, logits - top, 0.0)), 0.0)
+    mine = lax.broadcasted_iota(jnp.int32, weight.shape, 1) == me
+    share = jnp.sum(jnp.where(mine, weight, 0.0), axis=1, keepdims=True)
+    gates = share / jnp.sum(weight, axis=1, keepdims=True)
+
+    step = 256
+    for j in range(0, ff, step):
+        g = jnp.dot(rows[:, 0:D], gate_v[:, j : j + step], preferred_element_type=jnp.float32)
+        u = jnp.dot(rows[:, 0:D], up_v[:, j : j + step], preferred_element_type=jnp.float32)
+        act[:, j : j + step] = (g / (1.0 + jnp.exp(-g)) * u).astype(jnp.bfloat16)
+
+    core_back = [
+        remote(core_out.at[q], core_in.at[q], rc_s.at[q], rc_r.at[q], core_peer) for q in range(Q)
+    ]
+    y_back = [remote(y_out.at[q], y_in.at[q], ry_s.at[q], ry_r.at[q], y_peer) for q in range(Q)]
+    z_back = [
+        [
+            remote(z_out.at[q, s - 1], z_in.at[q, s - 1], rz_s.at[q, s - 1], rz_r.at[q, s - 1], z_peer(s))
+            for s in range(1, Z)
+        ]
+        for q in range(Q)
+    ]
+
+    def first(q):
+        o = jnp.dot(act[...], down_v[:, q * cols : (q + 1) * cols], preferred_element_type=jnp.float32)
+        o = o * gates
+        core_out[q] = o[half:].astype(jnp.bfloat16)
+        keep[q] = o[:half]
+        core_back[q].start()
+
+    def second(q):
+        core_back[q].wait_recv()
+        total = keep[q] + core_in[q].astype(jnp.float32)
+        y_out[q] = total[quarter:].astype(jnp.bfloat16)
+        keep[q, 0:quarter] = total[:quarter]
+        y_back[q].start()
+
+    def third(q):
+        y_back[q].wait_recv()
+        total = keep[q, 0:quarter] + y_in[q].astype(jnp.float32)
+        for s in range(1, Z):
+            z_out[q, s - 1] = total[s * R : (s + 1) * R].astype(jnp.bfloat16)
+            z_back[q][s - 1].start()
+        keep[q, 0:R] = total[:R]
+
+    def last(q):
+        total = keep[q, 0:R]
+        for s in range(1, Z):
+            z_back[q][s - 1].wait_recv()
+            total = total + z_in[q, s - 1].astype(jnp.float32)
+        out[:, q * cols : (q + 1) * cols] = total.astype(jnp.bfloat16)
+
+    for t in range(Q + 3):
+        for lag, stage in enumerate((first, second, third, last)):
+            if 0 <= t - lag < Q:
+                stage(t - lag)
+    for copy in along_z + across_y + to_core + core_back + y_back + sum(z_back, []):
+        copy.wait_send()
+
+
+def gather_plan(tokens, router_weight, w_gate, w_up, w_down, expert_ids):
+    devices = lax.axis_size("exp")
+    R, D = tokens.shape
+    Z, Q = devices // 4, 4
+    experts = router_weight.shape[1]
+    ff = w_gate.shape[2]
+    total, half, quarter, cols = devices * R, devices * R // 2, devices * R // 4, D // Q
+    bf, f32, dma = jnp.bfloat16, jnp.float32, pltpu.SemaphoreType.DMA
+    return pl.pallas_call(
+        functools.partial(moe_kernel, Z, Q),
+        out_shape=jax.ShapeDtypeStruct((R, D), bf),
+        in_specs=[pl.BlockSpec(memory_space=pl.ANY)] * 6,
+        out_specs=pl.BlockSpec(memory_space=pltpu.VMEM),
+        scratch_shapes=[
+            pltpu.VMEM((total, D + LANES), bf),
+            pltpu.VMEM(expert_ids.shape[::-1], jnp.int32),
+            pltpu.VMEM((experts, D), bf),
+            pltpu.VMEM((D, ff), bf),
+            pltpu.VMEM((D, ff), bf),
+            pltpu.VMEM((ff, D), bf),
+            pltpu.VMEM((total, ff), bf),
+            pltpu.VMEM((Q, half, cols), f32),
+            pltpu.VMEM((Q, half, cols), bf),
+            pltpu.VMEM((Q, half, cols), bf),
+            pltpu.VMEM((Q, quarter, cols), bf),
+            pltpu.VMEM((Q, quarter, cols), bf),
+            pltpu.VMEM((Q, Z - 1, R, cols), bf),
+            pltpu.VMEM((Q, Z - 1, R, cols), bf),
+            dma((6,)),
+            dma((Z,)), dma((Z,)), dma((Z,)), dma((Z,)), dma((2 * Z,)), dma((2 * Z,)),
+            dma((Q,)), dma((Q,)), dma((Q,)), dma((Q,)), dma((Q, Z - 1)), dma((Q, Z - 1)),
+        ],
+        compiler_params=pltpu.CompilerParams(
+            collective_id=0, has_side_effects=True, vmem_limit_bytes=48 * 1024 * 1024
+        ),
+    )(tokens, router_weight.T, expert_ids.T, w_gate, w_up, w_down)
+
+
+def on_device(tokens, router_weight, w_gate, w_up, w_down, expert_ids):
+    devices = lax.axis_size("exp")
+    tok_rows, chosen = expert_ids.shape
+    experts = devices * w_gate.shape[0]
+    capacity = min(tok_rows, max(2, (3 * tok_rows * chosen + 2 * experts - 1) // (2 * experts)))
+    args = (tokens, router_weight, w_gate, w_up, w_down, expert_ids)
+    if tok_rows <= 2 * capacity:
+        return gather_plan(*args)
+    return dispatch_plan(*args, capacity)
+
+
 def solution(mesh):
     placed = (
         P(("grp", "exp"), None),

time: 85.9 us -> 40.9 us (0.48); the launches traced: 84.4 us -> 40.6 us
  Pallas kernels: 0 us -> 35.7 us
  blocking collectives: 32 us -> 0 us
  waiting for transfers between devices: 21 us -> 0 us
  local copies, waits for them, and re-layouts: 17.8 us -> 4.89 us
  matrix products: 7.85 us -> 0 us
  starting transfers between devices: 5.04 us -> 0 us
    pallas_call x0 -> x1, Pallas kernels: none -> 35.7 us  [gather_plan(): pl.pallas_call(functools.partial(moe_kernel, Z, Q), out_shape=jax.ShapeDt...]
    all_to_all x1 -> x0, blocking collectives: 32 us -> none  [on_device(): lax.all_to_all(filled.reshape(capacity, experts, width), 'exp', split_axi...]
    all_to_all x1 -> x0, waiting for transfers between devices: 21 us -> none  [on_device(): lax.all_to_all(outs.reshape(count, experts, width), 'exp', split_axis=1,...]
    dot_general x4 -> x0, matrix products: 7.85 us -> none  [the longest x1 4.8 us: expert_rows(): jnp.dot(act, down_mat, preferred_element_type=jnp.float32)]
    gather x6 -> x0, local copies, waits for them, and re-layouts: 5.06 us -> none  [the longest x1 3.46 us: on_device(): back.reshape(capacity * experts, width)[place]]
    all_to_all x1 -> x0, starting transfers between devices: 5.04 us -> none  [on_device(): lax.all_to_all(outs.reshape(count, experts, width), 'exp', split_axis=1,...]
    reshape x3 -> x0, local copies, waits for them, and re-layouts: 4.47 us -> none  [the longest x1 2.66 us: on_device(): outs.reshape(count, experts, width)]
    unnamed x13 -> x9, local copies, waits for them, and re-layouts: 1.82 us -> 4.89 us
  transfers between devices with their start and end apart: 1 -> 0, of which waited for: 1 -> 0; matrix products, arithmetic and copies ran while one was open for 2% -> 0% of each run, Pallas kernels for 0% -> 0%
where the time goes in v1:
time: 40.9 us; the launch traced here: 40.6 us
  Pallas kernels  35.7 us (87%)
  local copies, waits for them, and re-layouts  4.89 us (12%)
    pallas_call x1, Pallas kernels, gather_plan(): pl.pallas_call(functools.partial(moe_kernel, Z, Q), out_shape=jax.ShapeDt...  35.7 us
    unnamed x9, local copies, waits for them, and re-layouts  4.89 us

profile of v1, /device:TPU:0, one launch (start us, length us, event | category | flops | bytes accessed | tf_op | source)
XLA Modules:
  0.0 40.6 jit_solution(5360255243087061741)
XLA Ops:
  0.0 0.0 copy-start
  0.0 1.9 %copy-done = bf16[1,2048,768]{2,1,0:T(8,128)(2,1)S(1)} copy-done((bf16[1,2048,768]{2,1,0:T(8,128)(2,1)S(1)}, bf16[1,2048,768]{2,1,0:T(8,128)(2,1)}, u32[]{:S(2)}) %copy-start) | copy-done | bytes 3145752
  1.9 0.0 copy-start.1
  1.9 0.8 %copy-done.1 = bf16[16,2048]{1,0:T(8,128)(2,1)S(1)} copy-done((bf16[16,2048]{1,0:T(8,128)(2,1)S(1)}, bf16[16,2048]{1,0:T(8,128)(2,1)}, u32[]{:S(2)}) %copy-start.1) | copy-done | bytes 65560
  2.7 0.0 copy-start.2
  2.7 0.8 %copy-done.2 = bf16[2048,16]{0,1:T(8,128)(2,1)S(1)} copy-done((bf16[2048,16]{0,1:T(8,128)(2,1)S(1)}, bf16[2048,16]{0,1:T(8,128)(2,1)}, u32[]{:S(2)}) %copy-start.2) | copy-done | bytes 65560
  3.6 0.0 copy-start.3
  3.6 0.7 %copy-done.3 = s32[16,8]{0,1:T(8,128)S(1)} copy-done((s32[16,8]{0,1:T(8,128)S(1)}, s32[16,8]{0,1:T(8,128)}, u32[]{:S(2)}) %copy-start.3) | copy-done | bytes 536
  4.3 35.7 %shard_map.64 = bf16[16,2048]{1,0:T(8,128)(2,1)S(1)} custom-call(bf16[16,2048]{1,0:T(8,128)(2,1)S(1)} %copy-done.1, bf16[16,2048]{1,0:T(8,128)(2,1)S(1)} %bitcast.2, s32[8,16]{1,0:T(8,128)S(1)} %bitcast.3, bf16[1,2048,768]{2,1,0:T(8,128)(2,1)S(1)} %copy-done, bf16[1,2048,768]{2,1,0:T(8,128)(2,1)} %w_up.1, bf16[1,768,2048]{2,1,0:T(8,128)(2,1)} %w_down.1), custom_call_target="tpu_custom_call" | custom-call | tf_op jit(solution)/shard_map/pallas_call | solution.py:201
  40.0 0.6 %copy.8 = bf16[16,2048]{1,0:T(8,128)(2,1)} copy(bf16[16,2048]{1,0:T(8,128)(2,1)S(1)} %shard_map.64) | data formatting | bytes 131072
Async XLA Ops:
  0.0 1.9 %copy-start = (bf16[1,2048,768]{2,1,0:T(8,128)(2,1)S(1)}, bf16[1,2048,768]{2,1,0:T(8,128)(2,1)}, u32[]{:S(2)}) copy-start(bf16[1,2048,768]{2,1,0:T(8,128)(2,1)} %w_gate.1) | copy-start | bytes 9437188
  1.9 0.8 %copy-start.1 = (bf16[16,2048]{1,0:T(8,128)(2,1)S(1)}, bf16[16,2048]{1,0:T(8,128)(2,1)}, u32[]{:S(2)}) copy-start(bf16[16,2048]{1,0:T(8,128)(2,1)} %tok.1) | copy-start | bytes 196612
  2.7 0.8 %copy-start.2 = (bf16[2048,16]{0,1:T(8,128)(2,1)S(1)}, bf16[2048,16]{0,1:T(8,128)(2,1)}, u32[]{:S(2)}) copy-start(bf16[2048,16]{0,1:T(8,128)(2,1)} %param.7) | copy-start | bytes 196612
  3.6 0.7 %copy-start.3 = (s32[16,8]{0,1:T(8,128)S(1)}, s32[16,8]{0,1:T(8,128)}, u32[]{:S(2)}) copy-start(s32[16,8]{0,1:T(8,128)} %param.11) | copy-start | bytes 1540

commit v2 on v1

--- a/solution.py
+++ b/solution.py
@@ -46,7 +46,7 @@
 
 
 def moe_kernel(
-    Z, Q, tok, router, ids, w_gate, w_up, w_down, out,
+    Z, Q, G, tok, router, ids, w_gate, w_up, w_down, out,
     rows, ids_v, router_v, gate_v, up_v, down_v, act,
     keep, core_out, core_in, y_out, y_in, z_out, z_in,
     load_sem, gz_s, gz_r, gy_s, gy_r, gc_s, gc_r,
@@ -70,9 +70,6 @@
             src_ref=src, dst_ref=dst, send_sem=send, recv_sem=recv,
             device_id=peer, device_id_type=MESH,
         )
-
-    def slot(i, n=1):
-        return rows.at[pl.ds(i * R, n * R)]
 
     loads = [
         pltpu.make_async_copy(ids, ids_v, load_sem.at[0]),
@@ -98,29 +95,44 @@
     loads[1].wait()
     pl.semaphore_wait(barrier, Z + 1)
 
+    tiles = rows.shape[1] // LANES
+    edges = [(tiles * g + G - 1) // G * LANES for g in range(G + 1)]
+
+    def slots(i, n, g):
+        return rows.at[pl.ds(i * R, n * R), pl.ds(edges[g], edges[g + 1] - edges[g])]
+
     along_z = [
-        remote(slot(0), slot(s), gz_s.at[s], gz_r.at[s], z_peer(Z - s)) for s in range(1, Z)
+        [remote(slots(0, 1, g), slots(s, 1, g), gz_s.at[g, s], gz_r.at[g, s], z_peer(Z - s)) for s in range(Z)]
+        for g in range(G)
     ]
     across_y = [
-        remote(slot(s), slot(Z + s), gy_s.at[s], gy_r.at[s], y_peer) for s in range(Z)
+        [remote(slots(s, 1, g), slots(Z + s, 1, g), gy_s.at[g, s], gy_r.at[g, s], y_peer) for s in range(Z)]
+        for g in range(G)
     ]
     to_core = [
-        remote(slot(s), slot(2 * Z + s), gc_s.at[s], gc_r.at[s], core_peer) for s in range(2 * Z)
-    ]
-    order = [0] + sorted(range(1, Z), key=lambda s: min(s, Z - s))
-    for s in order[1:]:
-        along_z[s - 1].start()
-    across_y[0].start()
-    to_core[0].start()
-    for s in order[1:]:
-        along_z[s - 1].wait_recv()
-        across_y[s].start()
-        to_core[s].start()
-    for s in order:
-        across_y[s].wait_recv()
-        to_core[Z + s].start()
-    for copy in to_core:
-        copy.wait_recv()
+        [
+            remote(slots(h * Z, Z, g), slots((2 + h) * Z, Z, g), gc_s.at[g, h], gc_r.at[g, h], core_peer)
+            for h in range(2)
+        ]
+        for g in range(G)
+    ]
+    order = sorted(range(1, Z), key=lambda s: min(s, Z - s))
+    for g in range(G):
+        across_y[g][0].start()
+        for s in order:
+            along_z[g][s].start()
+    for g in range(G):
+        for s in order:
+            along_z[g][s].wait_recv()
+            across_y[g][s].start()
+        to_core[g][0].start()
+    for g in range(G):
+        for s in [0] + order:
+            across_y[g][s].wait_recv()
+        to_core[g][1].start()
+    for g in range(G):
+        for h in range(2):
+            to_core[g][h].wait_recv()
 
     for load in loads[2:]:
         load.wait()
@@ -182,26 +194,31 @@
             total = total + z_in[q, s - 1].astype(jnp.float32)
         out[:, q * cols : (q + 1) * cols] = total.astype(jnp.bfloat16)
 
-    for t in range(Q + 3):
-        for lag, stage in enumerate((first, second, third, last)):
-            if 0 <= t - lag < Q:
-                stage(t - lag)
-    for copy in along_z + across_y + to_core + core_back + y_back + sum(z_back, []):
+    for q in range(Q + 1):
+        if q < Q:
+            first(q)
+        if q > 0:
+            second(q - 1)
+    for stage in (third, last):
+        for q in range(Q):
+            stage(q)
+    sent = [copy for g in range(G) for copy in along_z[g][1:] + across_y[g] + to_core[g]]
+    for copy in sent + core_back + y_back + sum(z_back, []):
         copy.wait_send()
 
 
 def gather_plan(tokens, router_weight, w_gate, w_up, w_down, expert_ids):
     devices = lax.axis_size("exp")
     R, D = tokens.shape
-    Z, Q = devices // 4, 4
+    Z, Q, G = devices // 4, 4, 4
     experts = router_weight.shape[1]
     ff = w_gate.shape[2]
     total, half, quarter, cols = devices * R, devices * R // 2, devices * R // 4, D // Q
     bf, f32, dma = jnp.bfloat16, jnp.float32, pltpu.SemaphoreType.DMA
     return pl.pallas_call(
-        functools.partial(moe_kernel, Z, Q),
+        functools.partial(moe_kernel, Z, Q, G),
         out_shape=jax.ShapeDtypeStruct((R, D), bf),
-        in_specs=[pl.BlockSpec(memory_space=pl.ANY)] * 6,
+        in_specs=[pl.BlockSpec(memory_space=pltpu.HBM)] * 6,
         out_specs=pl.BlockSpec(memory_space=pltpu.VMEM),
         scratch_shapes=[
             pltpu.VMEM((total, D + LANES), bf),
@@ -219,11 +236,11 @@
             pltpu.VMEM((Q, Z - 1, R, cols), bf),
             pltpu.VMEM((Q, Z - 1, R, cols), bf),
             dma((6,)),
-            dma((Z,)), dma((Z,)), dma((Z,)), dma((Z,)), dma((2 * Z,)), dma((2 * Z,)),
+            dma((G, Z)), dma((G, Z)), dma((G, Z)), dma((G, Z)), dma((G, 2)), dma((G, 2)),
             dma((Q,)), dma((Q,)), dma((Q,)), dma((Q,)), dma((Q, Z - 1)), dma((Q, Z - 1)),
         ],
         compiler_params=pltpu.CompilerParams(
-            collective_id=0, has_side_effects=True, vmem_limit_bytes=48 * 1024 * 1024
+            collective_id=0, has_side_effects=True, vmem_limit_bytes=60 * 1024 * 1024
         ),
     )(tokens, router_weight.T, expert_ids.T, w_gate, w_up, w_down)
 

time: 40.9 us -> 34.2 us (0.84)
  local copies, waits for them, and re-layouts: 4.89 us -> 1.47 us
  Pallas kernels: 35.7 us -> 32.5 us
    unnamed x9 -> x1, local copies, waits for them, and re-layouts: 4.89 us -> 1.47 us
    pallas_call x1, Pallas kernels: 35.7 us -> 32.5 us  [gather_plan(): pl.pallas_call(functools.partial(moe_kernel, Z, Q, G), out_shape=jax.Shap...]
where the time goes in v2:
time: 34.2 us; the launch traced here: 34 us
  Pallas kernels  32.5 us (95%)
  local copies, waits for them, and re-layouts  1.47 us (4%)
    pallas_call x1, Pallas kernels, gather_plan(): pl.pallas_call(functools.partial(moe_kernel, Z, Q, G), out_shape=jax.Shap...  32.5 us
    unnamed x1, local copies, waits for them, and re-layouts  1.47 us

profile of v2, /device:TPU:0, one launch (start us, length us, event | category | flops | bytes accessed | tf_op | source)
XLA Modules:
  0.0 34.0 jit_solution(1749421489041884229)
XLA Ops:
  0.0 32.5 %shard_map.64 = bf16[16,2048]{1,0:T(8,128)(2,1)} custom-call(bf16[16,2048]{1,0:T(8,128)(2,1)} %tok.1, bf16[16,2048]{1,0:T(8,128)(2,1)} %bitcast.2, s32[8,16]{1,0:T(8,128)} %bitcast.3, bf16[1,2048,768]{2,1,0:T(8,128)(2,1)} %w_gate.1, bf16[1,2048,768]{2,1,0:T(8,128)(2,1)} %w_up.1, bf16[1,768,2048]{2,1,0:T(8,128)(2,1)} %w_down.1), custom_call_target="tpu_custom_call" | custom-call | tf_op jit(solution)/shard_map/pallas_call | solution.py:218
  32.5 1.5 %copy.8 = bf16[16,2048]{1,0:T(8,128)(2,1)} copy(bf16[16,2048]{1,0:T(8,128)(2,1)} %shard_map.64) | data formatting | bytes 131072

commit v3 on v2

--- a/solution.py
+++ b/solution.py
@@ -106,12 +106,12 @@
         for g in range(G)
     ]
     across_y = [
-        [remote(slots(s, 1, g), slots(Z + s, 1, g), gy_s.at[g, s], gy_r.at[g, s], y_peer) for s in range(Z)]
+        [remote(slots(s, 1, g), slots(2 * Z + s, 1, g), gy_s.at[g, s], gy_r.at[g, s], y_peer) for s in range(Z)]
         for g in range(G)
     ]
     to_core = [
         [
-            remote(slots(h * Z, Z, g), slots((2 + h) * Z, Z, g), gc_s.at[g, h], gc_r.at[g, h], core_peer)
+            remote(slots(2 * h * Z, Z, g), slots((2 * h + 1) * Z, Z, g), gc_s.at[g, h], gc_r.at[g, h], core_peer)
             for h in range(2)
         ]
         for g in range(G)
@@ -126,35 +126,40 @@
             along_z[g][s].wait_recv()
             across_y[g][s].start()
         to_core[g][0].start()
+
+    def hidden(h):
+        mine = slice(h * half, (h + 1) * half)
+        logits = lax.dot_general(
+            rows[mine, 0:D], router_v[...], (((1,), (1,)), ((), ())), preferred_element_type=jnp.float32
+        )
+        chosen = rows[mine, D : D + experts].astype(jnp.float32) > 0.5
+        top = jnp.max(jnp.where(chosen, logits, -jnp.inf), axis=1, keepdims=True)
+        weight = jnp.where(chosen, jnp.exp(jnp.where(chosen, logits - top, 0.0)), 0.0)
+        own = lax.broadcasted_iota(jnp.int32, weight.shape, 1) == me
+        share = jnp.sum(jnp.where(own, weight, 0.0), axis=1, keepdims=True)
+        step = 256
+        for j in range(0, ff, step):
+            g = jnp.dot(rows[mine, 0:D], gate_v[:, j : j + step], preferred_element_type=jnp.float32)
+            u = jnp.dot(rows[mine, 0:D], up_v[:, j : j + step], preferred_element_type=jnp.float32)
+            act[mine, j : j + step] = (g / (1.0 + jnp.exp(-g)) * u).astype(jnp.bfloat16)
+        return share / jnp.sum(weight, axis=1, keepdims=True)
+
+    for g in range(G):
+        to_core[g][0].wait_recv()
+    for load in loads[2:]:
+        load.wait()
+    gates = [hidden(0)]
     for g in range(G):
         for s in [0] + order:
             across_y[g][s].wait_recv()
         to_core[g][1].start()
     for g in range(G):
-        for h in range(2):
-            to_core[g][h].wait_recv()
-
-    for load in loads[2:]:
-        load.wait()
-    x = rows[:, 0:D]
-    logits = lax.dot_general(
-        x, router_v[...], (((1,), (1,)), ((), ())), preferred_element_type=jnp.float32
-    )
-    chosen = rows[:, D : D + experts].astype(jnp.float32) > 0.5
-    top = jnp.max(jnp.where(chosen, logits, -jnp.inf), axis=1, keepdims=True)
-    weight = jnp.where(chosen, jnp.exp(jnp.where(chosen, logits - top, 0.0)), 0.0)
-    mine = lax.broadcasted_iota(jnp.int32, weight.shape, 1) == me
-    share = jnp.sum(jnp.where(mine, weight, 0.0), axis=1, keepdims=True)
-    gates = share / jnp.sum(weight, axis=1, keepdims=True)
-
-    step = 256
-    for j in range(0, ff, step):
-        g = jnp.dot(rows[:, 0:D], gate_v[:, j : j + step], preferred_element_type=jnp.float32)
-        u = jnp.dot(rows[:, 0:D], up_v[:, j : j + step], preferred_element_type=jnp.float32)
-        act[:, j : j + step] = (g / (1.0 + jnp.exp(-g)) * u).astype(jnp.bfloat16)
+        to_core[g][1].wait_recv()
+    gates.append(hidden(1))
 
     core_back = [
-        remote(core_out.at[q], core_in.at[q], rc_s.at[q], rc_r.at[q], core_peer) for q in range(Q)
+        [remote(core_out.at[h, q], core_in.at[h, q], rc_s.at[h, q], rc_r.at[h, q], core_peer) for q in range(Q)]
+        for h in range(2)
     ]
     y_back = [remote(y_out.at[q], y_in.at[q], ry_s.at[q], ry_r.at[q], y_peer) for q in range(Q)]
     z_back = [
@@ -165,52 +170,54 @@
         for q in range(Q)
     ]
 
-    def first(q):
-        o = jnp.dot(act[...], down_v[:, q * cols : (q + 1) * cols], preferred_element_type=jnp.float32)
-        o = o * gates
-        core_out[q] = o[half:].astype(jnp.bfloat16)
-        keep[q] = o[:half]
-        core_back[q].start()
+    def first(h, q):
+        o = jnp.dot(
+            act[h * half : (h + 1) * half], down_v[:, q * cols : (q + 1) * cols],
+            preferred_element_type=jnp.float32,
+        )
+        o = o * gates[h]
+        core_out[h, q] = o[quarter:].astype(jnp.bfloat16)
+        keep[h, q] = o[:quarter]
+        core_back[h][q].start()
 
     def second(q):
-        core_back[q].wait_recv()
-        total = keep[q] + core_in[q].astype(jnp.float32)
-        y_out[q] = total[quarter:].astype(jnp.bfloat16)
-        keep[q, 0:quarter] = total[:quarter]
+        core_back[1][q].wait_recv()
+        y_out[q] = (keep[1, q] + core_in[1, q].astype(jnp.float32)).astype(jnp.bfloat16)
         y_back[q].start()
 
     def third(q):
+        core_back[0][q].wait_recv()
         y_back[q].wait_recv()
-        total = keep[q, 0:quarter] + y_in[q].astype(jnp.float32)
+        total = keep[0, q] + core_in[0, q].astype(jnp.float32) + y_in[q].astype(jnp.float32)
         for s in range(1, Z):
             z_out[q, s - 1] = total[s * R : (s + 1) * R].astype(jnp.bfloat16)
             z_back[q][s - 1].start()
-        keep[q, 0:R] = total[:R]
+        keep[0, q, 0:R] = total[:R]
 
     def last(q):
-        total = keep[q, 0:R]
+        total = keep[0, q, 0:R]
         for s in range(1, Z):
             z_back[q][s - 1].wait_recv()
             total = total + z_in[q, s - 1].astype(jnp.float32)
         out[:, q * cols : (q + 1) * cols] = total.astype(jnp.bfloat16)
 
-    for q in range(Q + 1):
-        if q < Q:
-            first(q)
-        if q > 0:
-            second(q - 1)
+    for q in range(Q):
+        first(1, q)
+    for q in range(Q):
+        second(q)
+        first(0, q)
     for stage in (third, last):
         for q in range(Q):
             stage(q)
     sent = [copy for g in range(G) for copy in along_z[g][1:] + across_y[g] + to_core[g]]
-    for copy in sent + core_back + y_back + sum(z_back, []):
+    for copy in sent + sum(core_back, []) + y_back + sum(z_back, []):
         copy.wait_send()
 
 
 def gather_plan(tokens, router_weight, w_gate, w_up, w_down, expert_ids):
     devices = lax.axis_size("exp")
     R, D = tokens.shape
-    Z, Q, G = devices // 4, 4, 4
+    Z, Q, G = devices // 4, 4, 2
     experts = router_weight.shape[1]
     ff = w_gate.shape[2]
     total, half, quarter, cols = devices * R, devices * R // 2, devices * R // 4, D // Q
@@ -228,16 +235,16 @@
             pltpu.VMEM((D, ff), bf),
             pltpu.VMEM((ff, D), bf),
             pltpu.VMEM((total, ff), bf),
-            pltpu.VMEM((Q, half, cols), f32),
-            pltpu.VMEM((Q, half, cols), bf),
-            pltpu.VMEM((Q, half, cols), bf),
+            pltpu.VMEM((2, Q, quarter, cols), f32),
+            pltpu.VMEM((2, Q, quarter, cols), bf),
+            pltpu.VMEM((2, Q, quarter, cols), bf),
             pltpu.VMEM((Q, quarter, cols), bf),
             pltpu.VMEM((Q, quarter, cols), bf),
             pltpu.VMEM((Q, Z - 1, R, cols), bf),
             pltpu.VMEM((Q, Z - 1, R, cols), bf),
             dma((6,)),
             dma((G, Z)), dma((G, Z)), dma((G, Z)), dma((G, Z)), dma((G, 2)), dma((G, 2)),
-            dma((Q,)), dma((Q,)), dma((Q,)), dma((Q,)), dma((Q, Z - 1)), dma((Q, Z - 1)),
+            dma((2, Q)), dma((2, Q)), dma((Q,)), dma((Q,)), dma((Q, Z - 1)), dma((Q, Z - 1)),
         ],
         compiler_params=pltpu.CompilerParams(
             collective_id=0, has_side_effects=True, vmem_limit_bytes=60 * 1024 * 1024

time: 34.2 us -> 33.5 us (0.980)
  Pallas kernels: 32.5 us -> 31.8 us
    pallas_call x1, Pallas kernels: 32.5 us -> 31.8 us  [gather_plan(): pl.pallas_call(functools.partial(moe_kernel, Z, Q, G), out_shape=jax.Shap...]
where the time goes in v3:
time: 33.5 us; the launch traced here: 33.3 us
  Pallas kernels  31.8 us (95%)
  local copies, waits for them, and re-layouts  1.47 us (4%)
    pallas_call x1, Pallas kernels, gather_plan(): pl.pallas_call(functools.partial(moe_kernel, Z, Q, G), out_shape=jax.Shap...  31.8 us
    unnamed x1, local copies, waits for them, and re-layouts  1.47 us

profile of v3, /device:TPU:0, one launch (start us, length us, event | category | flops | bytes accessed | tf_op | source)
XLA Modules:
  0.0 33.3 jit_solution(1360609196868398940)
XLA Ops:
  0.0 31.8 %shard_map.64 = bf16[16,2048]{1,0:T(8,128)(2,1)} custom-call(bf16[16,2048]{1,0:T(8,128)(2,1)} %tok.1, bf16[16,2048]{1,0:T(8,128)(2,1)} %bitcast.2, s32[8,16]{1,0:T(8,128)} %bitcast.3, bf16[1,2048,768]{2,1,0:T(8,128)(2,1)} %w_gate.1, bf16[1,2048,768]{2,1,0:T(8,128)(2,1)} %w_up.1, bf16[1,768,2048]{2,1,0:T(8,128)(2,1)} %w_down.1), custom_call_target="tpu_custom_call" | custom-call | tf_op jit(solution)/shard_map/pallas_call | solution.py:225
  31.8 1.5 %copy.8 = bf16[16,2048]{1,0:T(8,128)(2,1)} copy(bf16[16,2048]{1,0:T(8,128)(2,1)} %shard_map.64) | data formatting | bytes 131072

commit v4 on v3

--- a/solution.py
+++ b/solution.py
@@ -217,7 +217,7 @@
 def gather_plan(tokens, router_weight, w_gate, w_up, w_down, expert_ids):
     devices = lax.axis_size("exp")
     R, D = tokens.shape
-    Z, Q, G = devices // 4, 4, 2
+    Z, Q, G = devices // 4, 4, 1
     experts = router_weight.shape[1]
     ff = w_gate.shape[2]
     total, half, quarter, cols = devices * R, devices * R // 2, devices * R // 4, D // Q

time: 33.5 us -> 33.7 us (level)
  no operation moved by 1% of the time
where the time goes in v4:
time: 33.7 us; the launch traced here: 33.5 us
  Pallas kernels  32 us (95%)
  local copies, waits for them, and re-layouts  1.47 us (4%)
    pallas_call x1, Pallas kernels, gather_plan(): pl.pallas_call(functools.partial(moe_kernel, Z, Q, G), out_shape=jax.Shap...  32 us
    unnamed x1, local copies, waits for them, and re-layouts  1.47 us

profile of v4, /device:TPU:0, one launch (start us, length us, event | category | flops | bytes accessed | tf_op | source)
XLA Modules:
  0.0 33.5 jit_solution(10954031011190476207)
XLA Ops:
  0.0 32.0 %shard_map.64 = bf16[16,2048]{1,0:T(8,128)(2,1)} custom-call(bf16[16,2048]{1,0:T(8,128)(2,1)} %tok.1, bf16[16,2048]{1,0:T(8,128)(2,1)} %bitcast.2, s32[8,16]{1,0:T(8,128)} %bitcast.3, bf16[1,2048,768]{2,1,0:T(8,128)(2,1)} %w_gate.1, bf16[1,2048,768]{2,1,0:T(8,128)(2,1)} %w_up.1, bf16[1,768,2048]{2,1,0:T(8,128)(2,1)} %w_down.1), custom_call_target="tpu_custom_call" | custom-call | tf_op jit(solution)/shard_map/pallas_call | solution.py:225
  32.0 1.5 %copy.8 = bf16[16,2048]{1,0:T(8,128)(2,1)} copy(bf16[16,2048]{1,0:T(8,128)(2,1)} %shard_map.64) | data formatting | bytes 131072
